TPU v7x, 256 devices: a whole 4x4x8 slice. The times are simulated.
256 devices in a mesh: sub: 16 (over z, core), row: 16 (over y, x).
Axes of the slice: x: 4, y: 4, z: 8, core: 2. Of those that a mesh axis runs over, the one named last changes fastest.
Arguments:
- modes: float32 [196608, 64], P(('sub', 'row')), may hold values from -6 to 6
- search: float32 [196608, 64], P(('sub', 'row')), may hold values from -6 to 6
- precond: float32 [196608], P(('sub', 'row')), may hold values from 0.05 to 0.25
- in_row: int32 [16, 16, 96], P('sub', 'row'), may hold values from 0 to 11, as said below
- in_col: int32 [16, 16, 96], P('sub', 'row'), may hold values from 0 to 191, as said below
- in_val: bfloat16 [16, 16, 96, 64, 64], P('sub', 'row'), as said below
- bnd_rows: int32 [16, 16, 3], P('sub', 'row'), may hold values from 0 to 11, as said below
- if_row: int32 [16, 16, 12], P('sub', 'row'), may hold values from 0 to 11, as said below
- if_src: int32 [16, 16, 12], P('sub', 'row'), may hold values from 0 to 47, as said below
- if_val: bfloat16 [16, 16, 12, 64, 64], P('sub', 'row')
Outputs:
- modes_out: float32 [196608, 64], P(('sub', 'row'))
- search_out: float32 [196608, 64], P(('sub', 'row'))
Inputs may be any that keep to these rules, and one draw needn't show every extreme that they name: `in_row`: entry k < 12 is k; each later group of 12 entries names each of the device's block-rows once. `in_col`: entry k < 12 is r * 12 + k on device (s, r); in each later group of 12 entries the devices of a subdomain together name each of its 192 block-rows once, and no entry names its own block-row. `in_val`: the first 12 blocks of every device are symmetric; the operator A is symmetric positive definite. `bnd_rows`: distinct within a device. `if_row`: each of the device's 12 block-rows once. `if_src`: t * 3 + q with t never the device's own subdomain; among the devices with one index of row, each boundary slot of each subdomain is named exactly 4 times.
All inputs are finite; a program needn't handle non-finite values.
Results may differ from a plain program's by a relative error of at most 0.0006.
Values may be sent and summed in bfloat16 or wider, within the bound.
A program may use at most 128 MiB of HBM per device.

v0:
```python
import jax
import jax.numpy as jnp
from jax import lax
from jax.sharding import PartitionSpec as P

KB = 64
LB = 12
ITERS = 2
IFR = 3
precise_mode = lax.Precision.HIGHEST


def gram_product(left, right):
    return jnp.dot(left.T, right, precision=precise_mode, preferred_element_type=jnp.float32)


def full_dot(left, right):
    return jnp.dot(left, right, precision=precise_mode, preferred_element_type=jnp.float32)


def chol_solve(matrix, rhs):
    factor = jnp.linalg.cholesky(matrix)
    halfway = lax.linalg.triangular_solve(factor, rhs, left_side=True, lower=True)
    return lax.linalg.triangular_solve(
        factor, halfway, left_side=True, lower=True, transpose_a=True
    )


def rescale(factor, moved):
    return lax.linalg.triangular_solve(factor, moved, left_side=False, lower=True, transpose_a=True)


def project(current, image_x):
    return lax.psum(
        (gram_product(current, current), gram_product(current, image_x)), ("sub", "row")
    )


def apply_blocks(vector, blocks):
    rows_here, cols_here, vals_here, bnd_here, face_rows, face_src, face_vals = blocks
    width = vector.shape[1]
    mine = vector.reshape(LB, KB, width)
    local_ids = jnp.arange(LB, dtype=jnp.int32)
    position = lax.axis_index("row")
    group = lax.all_gather(vector, "row", axis=0, tiled=True).reshape(-1, KB, width)
    forward = jnp.einsum("kij,kjw->kiw", vals_here, group[cols_here], precision=precise_mode)
    select = (rows_here[:, None] == local_ids[None, :]).astype(jnp.float32)
    result = jnp.einsum("ka,kiw->aiw", select, forward, precision=precise_mode)
    backward = jnp.einsum("kji,kjw->kiw", vals_here, mine[rows_here], precision=precise_mode)
    keeper = (cols_here != position * LB + rows_here).astype(jnp.float32)
    backward = backward * keeper[:, None, None]
    wanted = jnp.arange(LB * KB * lax.axis_size("row") // KB, dtype=jnp.int32)
    chosen = (cols_here[None, :] == wanted[:, None]).astype(jnp.float32)
    returned = lax.psum_scatter(
        jnp.einsum("bk,kiw->biw", chosen, backward, precision=precise_mode).reshape(
            LB * KB * lax.axis_size("row"), width
        ),
        "row",
        scatter_dimension=0,
        tiled=True,
    )
    result = result + returned.reshape(LB, KB, width)
    boundary = mine[bnd_here].reshape(-1, width)
    remote = lax.all_gather(boundary, "sub", axis=0, tiled=True).reshape(-1, KB, width)
    forward = jnp.einsum("kij,kjw->kiw", face_vals, remote[face_src], precision=precise_mode)
    face_select = (face_rows[:, None] == local_ids[None, :]).astype(jnp.float32)
    result = result + jnp.einsum("ka,kiw->aiw", face_select, forward, precision=precise_mode)
    backward = jnp.einsum("kji,kjw->kiw", face_vals, mine[face_rows], precision=precise_mode)
    wanted = jnp.arange(IFR * KB * lax.axis_size("sub") // KB, dtype=jnp.int32)
    chosen = (face_src[None, :] == wanted[:, None]).astype(jnp.float32)
    landed = lax.psum_scatter(
        jnp.einsum("bk,kiw->biw", chosen, backward, precision=precise_mode).reshape(
            IFR * KB * lax.axis_size("sub"), width
        ),
        "sub",
        scatter_dimension=0,
        tiled=True,
    ).reshape(IFR, KB, width)
    placed = (bnd_here[:, None] == local_ids[None, :]).astype(jnp.float32)
    result = result + jnp.einsum("qa,qiw->aiw", placed, landed, precision=precise_mode)
    return result.reshape(LB * KB, width)


def local(modes, search, precond, in_row, in_col, in_val, bnd_rows, if_row, if_src, if_val):
    blocks = (
        in_row[0, 0],
        in_col[0, 0],
        in_val[0, 0].astype(jnp.float32),
        bnd_rows[0, 0],
        if_row[0, 0],
        if_src[0, 0],
        if_val[0, 0].astype(jnp.float32),
    )
    total_rows = modes.shape[0] * lax.axis_size("sub") * lax.axis_size("row")
    nmode = modes.shape[1]
    images = apply_blocks(jnp.concatenate([modes, search], 1), blocks)
    current, direction = (modes, search)
    image_x, image_p = (images[:, :nmode], images[:, nmode:])
    for sweep in range(ITERS):
        correlation, energy = project(current, image_x)
        ritz = chol_solve(correlation, energy)
        residue = image_x - full_dot(current, ritz)
        update = precond[:, None] * residue
        image_w = apply_blocks(update, blocks)
        basis = jnp.concatenate([update, direction], 1)
        image_b = jnp.concatenate([image_w, image_p], 1)
        coupled, driving = lax.psum(
            (gram_product(basis, image_b), gram_product(basis, image_x)), ("sub", "row")
        )
        coeffs = -chol_solve(coupled, driving)
        step_x = full_dot(basis, coeffs)
        step_a = full_dot(image_b, coeffs)
        moved = current + step_x
        moved_image = image_x + step_a
        lengths = lax.psum(gram_product(moved, moved), ("sub", "row"))
        factor = jnp.linalg.cholesky(lengths / total_rows)
        current = rescale(factor, moved)
        image_x = rescale(factor, moved_image)
        direction = rescale(factor, step_x)
        image_p = rescale(factor, step_a)
    return (current, direction)


def solution(mesh):
    return jax.shard_map(
        local,
        mesh=mesh,
        in_specs=(
            P(("sub", "row"), None),
            P(("sub", "row"), None),
            P(("sub", "row")),
            P("sub", "row", None),
            P("sub", "row", None),
            P("sub", "row", None, None, None),
            P("sub", "row", None),
            P("sub", "row", None),
            P("sub", "row", None),
            P("sub", "row", None, None, None),
        ),
        out_specs=(P(("sub", "row"), None), P(("sub", "row"), None)),
        check_vma=False,
    )
```

profile of v0, /device:TPU:1, one launch (start us, length us, event | category | flops | bytes accessed | tf_op | source)
XLA Modules:
  0.0 1590.2 jit_solution(9537704448237477838)
XLA Ops:
  41.8 13.2 all-gather.9.cloned.1.call-done
  57.4 53.8 %reduce-scatter.13.cloned.1.call-done = f32[192,128]{1,0:T(8,128)} async-done(((f32[3072,128]{1,0:T(8,128)}), f32[192,128]{1,0:T(8,128)}) %reduce-scatter.13.cloned.1.call-update) | async-done | bytes 98320 | tf_op jit(solution)/shard_map/reduce_scatter | solution.py:71
  112.6 69.1 %all-gather.7.cloned.1.call-done = f32[12288,128]{1,0:T(8,128)} async-done(((f32[768,128]{1,0:T(8,128)}), f32[12288,128]{1,0:T(8,128)}) %all-gather.7.cloned.1.call-update) | async-done | bytes 6291472 | tf_op jit(solution)/shard_map/all_gather | solution.py:45
  192.2 78.6 %reduce-scatter.11.cloned.1.call-done = f32[768,128]{1,0:T(8,128)} async-done(((f32[12288,128]{1,0:T(8,128)}), f32[768,128]{1,0:T(8,128)}) %reduce-scatter.11.cloned.1.call-update) | async-done | bytes 393232 | tf_op jit(solution)/shard_map/reduce_scatter | solution.py:54
  277.3 76.9 %all-reduce.1 = (f32[64,64]{0,1:T(8,128)S(1)}, f32[64,64]{0,1:T(8,128)S(1)}) all-reduce(f32[64,64]{0,1:T(8,128)S(1)} %convolution_bitcast_fusion.16, f32[64,64]{0,1:T(8,128)} %fusion.130), channel_id=1, replica_groups=mesh['sub'=16,'row'=16] {'sub','row'}, use_global_device_ids=true, to_apply=%region_5.0 | all-reduce | flops 8192 | bytes 65536 | tf_op jit(solution)/shard_map/psum | solution.py:34
  381.2 6.5 multiply_bitcast_fusion.1
  411.0 21.9 %all-gather = f32[16,192,64]{1,2,0:T(8,128)} all-gather(f32[1,192,64]{1,2,0:T(8,128)S(1)} %copy.168), channel_id=1, replica_groups=mesh['sub'=16,'row'=16] {'sub'}, dimensions={0}, use_global_device_ids=true | all-gather | bytes 835584 | tf_op jit(solution)/shard_map/all_gather | solution.py:64
  441.7 45.4 %all-gather.11.cloned.1.call-done = f32[12288,64]{0,1:T(8,128)} async-done(((f32[768,64]{0,1:T(8,128)}), f32[12288,64]{0,1:T(8,128)}) %all-gather.11.cloned.1.call-update) | async-done | bytes 3145744 | tf_op jit(solution)/shard_map/all_gather | solution.py:45
  509.1 60.1 %reduce-scatter.15.cloned.1.call-done = f32[768,64]{0,1:T(8,128)} async-done(((f32[12288,64]{0,1:T(8,128)}), f32[768,64]{0,1:T(8,128)}) %reduce-scatter.15.cloned.1.call-update) | async-done | bytes 196624 | tf_op jit(solution)/shard_map/reduce_scatter | solution.py:54
  582.2 77.9 %psum.73 = f32[128,64]{0,1:T(8,128)S(1)} all-reduce(f32[128,64]{0,1:T(8,128)} %fusion.27), channel_id=1, replica_groups=mesh['sub'=16,'row'=16] {'sub','row'}, use_global_device_ids=true, to_apply=%region_11.16 | all-reduce | flops 8192 | bytes 65536 | tf_op jit(solution)/shard_map/psum | solution.py:107
  660.1 160.0 %all-reduce.5.cloned.1.call-done = f32[128,128]{0,1:T(8,128)} async-done(((f32[128,128]{0,1:T(8,128)}), f32[128,128]{0,1:T(8,128)}) %all-reduce.5.cloned.1.call-update) | async-done | bytes 65552 | tf_op jit(solution)/shard_map/psum | solution.py:107
  821.9 11.7 cholesky.127
  835.0 9.8 custom-call.31
  847.9 74.6 %psum.74 = f32[64,64]{0,1:T(8,128)S(1)} all-reduce(f32[64,64]{0,1:T(8,128)S(1)} %fusion.131), channel_id=1, replica_groups=mesh['sub'=16,'row'=16] {'sub','row'}, use_global_device_ids=true, to_apply=%region_12.19 | all-reduce | flops 4096 | bytes 32768 | tf_op jit(solution)/shard_map/psum | solution.py:115
  937.0 74.2 %all-reduce = (f32[64,64]{1,0:T(8,128)S(1)}, f32[64,64]{0,1:T(8,128)S(1)}) all-reduce(f32[64,64]{1,0:T(8,128)S(1)} %fusion.133, f32[64,64]{0,1:T(8,128)S(1)} %fusion.132), channel_id=1, replica_groups=mesh['sub'=16,'row'=16] {'sub','row'}, use_global_device_ids=true, to_apply=%region_14.22 | all-reduce | flops 8192 | bytes 65536 | tf_op jit(solution)/shard_map/psum | solution.py:34
  1034.0 6.6 multiply_bitcast_fusion
  1063.8 19.7 %all-gather.1 = f32[16,192,64]{1,2,0:T(8,128)S(1)} all-gather(f32[1,192,64]{1,2,0:T(8,128)S(1)} %copy.198), channel_id=1, replica_groups=mesh['sub'=16,'row'=16] {'sub'}, dimensions={0}, use_global_device_ids=true | all-gather | bytes 835584 | tf_op jit(solution)/shard_map/all_gather | solution.py:64
  1091.1 47.1 %all-gather.13.cloned.1.call-done = f32[12288,64]{0,1:T(8,128)} async-done(((f32[768,64]{0,1:T(8,128)}), f32[12288,64]{0,1:T(8,128)}) %all-gather.13.cloned.1.call-update) | async-done | bytes 3145744 | tf_op jit(solution)/shard_map/all_gather | solution.py:45
  1160.1 60.5 %reduce-scatter.17.cloned.1.call-done = f32[768,64]{0,1:T(8,128)} async-done(((f32[12288,64]{0,1:T(8,128)}), f32[768,64]{0,1:T(8,128)}) %reduce-scatter.17.cloned.1.call-update) | async-done | bytes 196624 | tf_op jit(solution)/shard_map/reduce_scatter | solution.py:54
  1229.7 77.7 %psum.78 = f32[128,64]{0,1:T(8,128)S(1)} all-reduce(f32[128,64]{0,1:T(8,128)S(1)} %fusion.25), channel_id=1, replica_groups=mesh['sub'=16,'row'=16] {'sub','row'}, use_global_device_ids=true, to_apply=%region_18.26 | all-reduce | flops 8192 | bytes 65536 | tf_op jit(solution)/shard_map/psum | solution.py:107
  1307.4 161.1 %all-reduce.7.cloned.1.call-done = f32[128,128]{0,1:T(8,128)} async-done(((f32[128,128]{0,1:T(8,128)}), f32[128,128]{0,1:T(8,128)}) %all-reduce.7.cloned.1.call-update) | async-done | bytes 65552 | tf_op jit(solution)/shard_map/psum | solution.py:107
  1470.3 11.7 cholesky.160
  1483.3 9.8 custom-call.39
  1494.3 74.6 %psum.79 = f32[64,64]{0,1:T(8,128)S(1)} all-reduce(f32[64,64]{0,1:T(8,128)S(1)} %fusion.134), channel_id=1, replica_groups=mesh['sub'=16,'row'=16] {'sub','row'}, use_global_device_ids=true, to_apply=%region_19.27 | all-reduce | flops 4096 | bytes 32768 | tf_op jit(solution)/shard_map/psum | solution.py:115
  (245 shorter events, 272.3 us)
Async XLA Ops:
  7.2 47.9 %all-gather.9.cloned.1.call-start = ((), (), s32[]{:S(2)}) async-start(), calls=%async_computation.8 | async-start | bytes 1671168 | tf_op jit(solution)/shard_map/all_gather | solution.py:64
  11.5 99.6 %reduce-scatter.13.cloned.1.call-start = ((), (), s32[]{:S(2)}) async-start(), calls=%async_computation.9 | async-start | bytes 1671168 | tf_op jit(solution)/shard_map/reduce_scatter | solution.py:71
  15.9 165.8 %all-gather.7.cloned.1.call-start = ((), (), s32[]{:S(2)}) async-start(), calls=%async_computation.6 | async-start | bytes 6684672 | tf_op jit(solution)/shard_map/all_gather | solution.py:45
  16.6 254.2 %reduce-scatter.11.cloned.1.call-start = ((), (), s32[]{:S(2)}) async-start(), calls=%async_computation.7 | async-start | bytes 6684672 | tf_op jit(solution)/shard_map/reduce_scatter | solution.py:54
  37.3 73.9 %copy-start.29 = (s32[1,1,3]{2,1,0:T(1,128)S(1)}, s32[1,1,3]{2,1,0:T(1,128)}, u32[]{:S(2)}) copy-start(s32[1,1,3]{2,1,0:T(1,128)} %param.28) | copy-start | bytes 40
  37.3 402.2 %reduce-scatter.19.cloned.1.call-start = ((), (), s32[]{:S(2)}) async-start(), calls=%async_computation.16 | async-start | bytes 1671168 | tf_op jit(solution)/shard_map/reduce_scatter | solution.py:71
  40.8 146.0 %copy-start.20 = (s32[1024]{0:T(1024)}, s32[1024]{0:T(1024)S(1)}, u32[]{:S(2)}) copy-start(s32[1024]{0:T(1024)S(1)} %pad_clamp_fusion.4) | copy-start | bytes 12292
  40.9 14.2 copy-start.23
  192.2 83.4 %copy-start.26 = (s32[1,1,12]{2,1,0:T(1,128)S(1)}, s32[1,1,12]{2,1,0:T(1,128)}, u32[]{:S(2)}) copy-start(s32[1,1,12]{2,1,0:T(1,128)} %param.29) | copy-start | bytes 148
  275.6 92.0 %copy-start.17 = (f32[768]{0:T(1024)S(1)}, f32[768]{0:T(1024)}, u32[]{:S(2)}) copy-start(f32[768]{0:T(1024)} %param.24) | copy-start | bytes 9220
  367.6 10.2 copy-start.13
  377.8 109.3 %all-gather.11.cloned.1.call-start = ((), (), s32[]{:S(2)}) async-start(), calls=%async_computation.10 | async-start | bytes 3342336 | tf_op jit(solution)/shard_map/all_gather | solution.py:45
  378.4 190.8 %reduce-scatter.15.cloned.1.call-start = ((), (), s32[]{:S(2)}) async-start(), calls=%async_computation.11 | async-start | bytes 3342336 | tf_op jit(solution)/shard_map/reduce_scatter | solution.py:54
  410.2 410.0 %all-reduce.5.cloned.1.call-start = ((), (), s32[]{:S(2)}) async-start(), calls=%async_computation.12 | async-start | bytes 131072 | tf_op jit(solution)/shard_map/psum | solution.py:107
  509.0 68.4 %copy-start.27 = (s32[1,1,12]{2,1,0:T(1,128)S(1)}, s32[1,1,12]{2,1,0:T(1,128)}, u32[]{:S(2)}) copy-start(s32[1,1,12]{2,1,0:T(1,128)} %param.29) | copy-start | bytes 148
  580.8 508.0 %reduce-scatter.21.cloned.1.call-start = ((), (), s32[]{:S(2)}) async-start(), calls=%async_computation.17 | async-start | bytes 1671168 | tf_op jit(solution)/shard_map/reduce_scatter | solution.py:71
  847.6 178.0 %copy-start.25 = (s32[1,1,12]{2,1,0:T(1,128)S(1)}, s32[1,1,12]{2,1,0:T(1,128)}, u32[]{:S(2)}) copy-start(s32[1,1,12]{2,1,0:T(1,128)} %param.30) | copy-start | bytes 148
  936.4 87.8 %copy-start.9 = (f32[768,64]{0,1:T(8,128)}, f32[768,64]{0,1:T(8,128)S(1)}, u32[]{:S(2)}) copy-start(f32[768,64]{0,1:T(8,128)S(1)} %convolution_bitcast_fusion.13) | copy-start | bytes 589828
  1030.8 107.3 %all-gather.13.cloned.1.call-start = ((), (), s32[]{:S(2)}) async-start(), calls=%async_computation.13 | async-start | bytes 3342336 | tf_op jit(solution)/shard_map/all_gather | solution.py:45
  1031.4 189.3 %reduce-scatter.17.cloned.1.call-start = ((), (), s32[]{:S(2)}) async-start(), calls=%async_computation.14 | async-start | bytes 3342336 | tf_op jit(solution)/shard_map/reduce_scatter | solution.py:54
  1063.0 405.5 %all-reduce.7.cloned.1.call-start = ((), (), s32[]{:S(2)}) async-start(), calls=%async_computation.15 | async-start | bytes 131072 | tf_op jit(solution)/shard_map/psum | solution.py:107
  1063.8 24.2 %copy-start.14 = (f32[768,64]{0,1:T(8,128)S(1)}, f32[768,64]{0,1:T(8,128)}, u32[]{:S(2)}) copy-start(f32[768,64]{0,1:T(8,128)} %fusion.42) | copy-start | bytes 589828
  1160.1 67.0 %copy-start.12 = (f32[12,64,64]{2,0,1:T(8,128)S(1)}, f32[12,64,64]{2,0,1:T(8,128)}, u32[]{:S(2)}) copy-start(f32[12,64,64]{2,0,1:T(8,128)} %fusion.36) | copy-start | bytes 589828
  1160.1 67.0 %copy-start.28 = (s32[1,1,12]{2,1,0:T(1,128)S(1)}, s32[1,1,12]{2,1,0:T(1,128)}, u32[]{:S(2)}) copy-start(s32[1,1,12]{2,1,0:T(1,128)} %param.29) | copy-start | bytes 148
  (19 other events, 90.9 us)
Sparse Core Ops, SparseCore 0:
  11.7 43.3 all-gather.8
  57.6 53.5 reduce-scatter.12
  113.9 67.7 all-gather.6
  185.7 85.0 reduce-scatter.10
  377.9 52.2 reduce-scatter.18
  433.1 53.9 all-gather.10
  490.7 78.4 reduce-scatter.14
  580.9 239.1 all-reduce.4
  1030.9 50.4 reduce-scatter.20
  1084.0 54.0 all-gather.12
  1142.2 78.3 reduce-scatter.16
  1229.3 239.1 all-reduce.6
where the time goes:
time: 1590 us
  waiting for transfers between devices  751 us (47%)
  blocking collectives  497 us (31%)
  local copies, waits for them, and re-layouts  128 us (8%)
  matrix products  100 us (6%)
  other arithmetic  97.2 us (6%)
    psum x2, waiting for transfers between devices, local(): lax.psum((gram_product(basis, image_b), gram_product(basis, image_x)), ('...  321 us
    reduce_scatter x6, waiting for transfers between devices, apply_blocks(): lax.psum_scatter(jnp.einsum('bk,kiw->biw', chosen, backward, precision=pr...  253 us
    all_gather x3, waiting for transfers between devices, apply_blocks(): lax.all_gather(vector, 'row', axis=0, tiled=True).reshape(-1, KB, width)  162 us
    psum x2, blocking collectives, local(): lax.psum((gram_product(basis, image_b), gram_product(basis, image_x)), ('...  156 us
    psum x2, blocking collectives, project(): lax.psum((gram_product(current, current), gram_product(current, image_x))...  151 us
    psum x2, blocking collectives, local(): lengths = lax.psum(gram_product(moved, moved), ('sub', 'row'))  149 us
    all_gather x2, blocking collectives, apply_blocks(): lax.all_gather(boundary, 'sub', axis=0, tiled=True).reshape(-1, KB, width)  41.6 us
    another operation x12, other arithmetic, chol_solve(): factor = jnp.linalg.cholesky(matrix)  37.8 us
  transfers between devices with their start and end apart: 12, of which 10 were waited for; matrix products, arithmetic and copies ran while one was open for 11% of the time, Pallas kernels for 0%

commit v1 on v0

--- a/solution.py
+++ b/solution.py
@@ -42,7 +42,9 @@
     mine = vector.reshape(LB, KB, width)
     local_ids = jnp.arange(LB, dtype=jnp.int32)
     position = lax.axis_index("row")
-    group = lax.all_gather(vector, "row", axis=0, tiled=True).reshape(-1, KB, width)
+    group = jnp.concatenate(
+        lax.all_to_all(jnp.stack([vector] * lax.axis_size("row")), "row", 0, 0), axis=0
+    ).reshape(-1, KB, width)
     forward = jnp.einsum("kij,kjw->kiw", vals_here, group[cols_here], precision=precise_mode)
     select = (rows_here[:, None] == local_ids[None, :]).astype(jnp.float32)
     result = jnp.einsum("ka,kiw->aiw", select, forward, precision=precise_mode)

time: 1590 us -> 1440 us (0.906)
  waiting for transfers between devices: 751 us -> 561 us
  starting transfers between devices: 1.4 us -> 17.7 us
    all_gather x3 -> x0, waiting for transfers between devices: 162 us -> none  [apply_blocks(): lax.all_gather(vector, 'row', axis=0, tiled=True).reshape(-1, KB, width)]
    reduce_scatter x6, waiting for transfers between devices: 253 us -> 176 us  [apply_blocks(): lax.psum_scatter(jnp.einsum('bk,kiw->biw', chosen, backward, precision=pr...]
    all_to_all x0 -> x3, waiting for transfers between devices: none -> 60.3 us  [apply_blocks(): lax.all_to_all(jnp.stack([vector] * lax.axis_size('row')), 'row', 0, 0)]
    all_to_all x0 -> x3, starting transfers between devices: none -> 17.1 us  [apply_blocks(): lax.all_to_all(jnp.stack([vector] * lax.axis_size('row')), 'row', 0, 0)]
  transfers between devices with their start and end apart: 12 -> 12, of which waited for: 10 -> 10; matrix products, arithmetic and copies ran while one was open for 11% -> 13% of each run, Pallas kernels for 0% -> 0%
where the time goes in v1:
time: 1440 us; the launch traced here: 1430 us
  waiting for transfers between devices  561 us (39%)
  blocking collectives  499 us (35%)
  local copies, waits for them, and re-layouts  141 us (10%)
  matrix products  100 us (7%)
  other arithmetic  97.2 us (7%)
  starting transfers between devices  17.7 us (1%)
  between operations  15.2 us (1%)
    psum x2, waiting for transfers between devices, local(): lax.psum((gram_product(basis, image_b), gram_product(basis, image_x)), ('...  321 us
    reduce_scatter x6, waiting for transfers between devices, apply_blocks(): lax.psum_scatter(jnp.einsum('bk,kiw->biw', chosen, backward, precision=pr...  176 us
    psum x2, blocking collectives, local(): lax.psum((gram_product(basis, image_b), gram_product(basis, image_x)), ('...  156 us
    psum x2, blocking collectives, project(): lax.psum((gram_product(current, current), gram_product(current, image_x))...  151 us
    psum x2, blocking collectives, local(): lengths = lax.psum(gram_product(moved, moved), ('sub', 'row'))  149 us
    all_to_all x3, waiting for transfers between devices, apply_blocks(): lax.all_to_all(jnp.stack([vector] * lax.axis_size('row')), 'row', 0, 0)  60.3 us
    all_gather x2, blocking collectives, apply_blocks(): lax.all_gather(boundary, 'sub', axis=0, tiled=True).reshape(-1, KB, width)  42.6 us
    another operation x12, other arithmetic, chol_solve(): factor = jnp.linalg.cholesky(matrix)  37.8 us
  transfers between devices with their start and end apart: 12, of which 10 were waited for; matrix products, arithmetic and copies ran while one was open for 13% of the time, Pallas kernels for 0%

profile of v1, /device:TPU:1, one launch (start us, length us, event | category | flops | bytes accessed | tf_op | source)
XLA Modules:
  0.0 1430.5 jit_solution(13826399754717218574)
XLA Ops:
  39.4 8.2 all-to-all-start
  57.4 55.7 %reduce-scatter.13.cloned.1.call-done = f32[192,128]{1,0:T(8,128)} async-done(((f32[3072,128]{1,0:T(8,128)}), f32[192,128]{1,0:T(8,128)}) %reduce-scatter.13.cloned.1.call-update) | async-done | bytes 98320 | tf_op jit(solution)/shard_map/reduce_scatter | solution.py:73
  114.5 28.5 %all-to-all-done = f32[16,768,128]{2,1,0:T(8,128)} async-done(((f32[16,768,128]{2,1,0:T(8,128)}), f32[16,768,128]{2,1,0:T(8,128)}, u32[]{:S(2)}, u32[]{:S(2)}) %all-to-all-start) | async-done | bytes 6291488 | tf_op jit(solution)/shard_map/all_to_all | solution.py:46
  153.7 52.9 %reduce-scatter.11.cloned.1.call-done = f32[768,128]{1,0:T(8,128)} async-done(((f32[12288,128]{1,0:T(8,128)}), f32[768,128]{1,0:T(8,128)}) %reduce-scatter.11.cloned.1.call-update) | async-done | bytes 393232 | tf_op jit(solution)/shard_map/reduce_scatter | solution.py:56
  213.8 77.0 %all-reduce.1 = (f32[64,64]{0,1:T(8,128)S(1)}, f32[64,64]{0,1:T(8,128)S(1)}) all-reduce(f32[64,64]{0,1:T(8,128)S(1)} %convolution_bitcast_fusion.16, f32[64,64]{0,1:T(8,128)S(1)} %fusion.130), channel_id=1, replica_groups=mesh['sub'=16,'row'=16] {'sub','row'}, use_global_device_ids=true, to_apply=%region_5.0 | all-reduce | flops 8192 | bytes 65536 | tf_op jit(solution)/shard_map/psum | solution.py:34
  316.5 6.5 multiply_bitcast_fusion.1
  352.7 21.6 %all-gather = f32[16,192,64]{1,2,0:T(8,128)} all-gather(f32[1,192,64]{1,2,0:T(8,128)S(1)} %copy.241), channel_id=1, replica_groups=mesh['sub'=16,'row'=16] {'sub'}, dimensions={0}, use_global_device_ids=true | all-gather | bytes 835584 | tf_op jit(solution)/shard_map/all_gather | solution.py:66
  384.7 16.1 %all-to-all-done.1 = f32[16,768,64]{1,2,0:T(8,128)} async-done(((f32[16,768,64]{1,2,0:T(8,128)}), f32[16,768,64]{1,2,0:T(8,128)}, u32[]{:S(2)}, u32[]{:S(2)}) %all-to-all-start.1) | async-done | bytes 3145760 | tf_op jit(solution)/shard_map/all_to_all | solution.py:46
  422.9 34.6 %reduce-scatter.15.cloned.1.call-done = f32[768,64]{0,1:T(8,128)} async-done(((f32[12288,64]{0,1:T(8,128)}), f32[768,64]{0,1:T(8,128)}) %reduce-scatter.15.cloned.1.call-update) | async-done | bytes 196624 | tf_op jit(solution)/shard_map/reduce_scatter | solution.py:56
  470.6 78.1 %psum.73 = f32[128,64]{0,1:T(8,128)S(1)} all-reduce(f32[128,64]{0,1:T(8,128)} %fusion.27), channel_id=1, replica_groups=mesh['sub'=16,'row'=16] {'sub','row'}, use_global_device_ids=true, to_apply=%region_11.16 | all-reduce | flops 8192 | bytes 65536 | tf_op jit(solution)/shard_map/psum | solution.py:109
  548.6 159.8 %all-reduce.5.cloned.1.call-done = f32[128,128]{0,1:T(8,128)} async-done(((f32[128,128]{0,1:T(8,128)}), f32[128,128]{0,1:T(8,128)}) %all-reduce.5.cloned.1.call-update) | async-done | bytes 65552 | tf_op jit(solution)/shard_map/psum | solution.py:109
  710.2 11.7 cholesky.127
  723.3 9.8 custom-call.31
  736.2 74.6 %psum.74 = f32[64,64]{0,1:T(8,128)S(1)} all-reduce(f32[64,64]{0,1:T(8,128)S(1)} %fusion.131), channel_id=1, replica_groups=mesh['sub'=16,'row'=16] {'sub','row'}, use_global_device_ids=true, to_apply=%region_12.19 | all-reduce | flops 4096 | bytes 32768 | tf_op jit(solution)/shard_map/psum | solution.py:117
  825.3 74.1 %all-reduce = (f32[64,64]{1,0:T(8,128)S(1)}, f32[64,64]{0,1:T(8,128)S(1)}) all-reduce(f32[64,64]{1,0:T(8,128)S(1)} %fusion.133, f32[64,64]{0,1:T(8,128)S(1)} %fusion.132), channel_id=1, replica_groups=mesh['sub'=16,'row'=16] {'sub','row'}, use_global_device_ids=true, to_apply=%region_14.22 | all-reduce | flops 8192 | bytes 65536 | tf_op jit(solution)/shard_map/psum | solution.py:34
  921.7 6.6 multiply_bitcast_fusion
  958.0 21.0 %all-gather.1 = f32[16,192,64]{1,2,0:T(8,128)} all-gather(f32[1,192,64]{1,2,0:T(8,128)S(1)} %copy.271), channel_id=1, replica_groups=mesh['sub'=16,'row'=16] {'sub'}, dimensions={0}, use_global_device_ids=true | all-gather | bytes 835584 | tf_op jit(solution)/shard_map/all_gather | solution.py:66
  990.2 15.7 %all-to-all-done.2 = f32[16,768,64]{1,2,0:T(8,128)} async-done(((f32[16,768,64]{1,2,0:T(8,128)}), f32[16,768,64]{1,2,0:T(8,128)}, u32[]{:S(2)}, u32[]{:S(2)}) %all-to-all-start.2) | async-done | bytes 3145760 | tf_op jit(solution)/shard_map/all_to_all | solution.py:46
  1028.1 32.9 %reduce-scatter.17.cloned.1.call-done = f32[768,64]{0,1:T(8,128)} async-done(((f32[12288,64]{0,1:T(8,128)}), f32[768,64]{0,1:T(8,128)}) %reduce-scatter.17.cloned.1.call-update) | async-done | bytes 196624 | tf_op jit(solution)/shard_map/reduce_scatter | solution.py:56
  1070.1 77.7 %psum.78 = f32[128,64]{0,1:T(8,128)S(1)} all-reduce(f32[128,64]{0,1:T(8,128)S(1)} %fusion.25), channel_id=1, replica_groups=mesh['sub'=16,'row'=16] {'sub','row'}, use_global_device_ids=true, to_apply=%region_18.26 | all-reduce | flops 8192 | bytes 65536 | tf_op jit(solution)/shard_map/psum | solution.py:109
  1147.7 161.1 %all-reduce.7.cloned.1.call-done = f32[128,128]{0,1:T(8,128)} async-done(((f32[128,128]{0,1:T(8,128)}), f32[128,128]{0,1:T(8,128)}) %all-reduce.7.cloned.1.call-update) | async-done | bytes 65552 | tf_op jit(solution)/shard_map/psum | solution.py:109
  1310.6 11.7 cholesky.160
  1323.7 9.8 custom-call.39
  1334.6 74.6 %psum.79 = f32[64,64]{0,1:T(8,128)S(1)} all-reduce(f32[64,64]{0,1:T(8,128)S(1)} %fusion.134), channel_id=1, replica_groups=mesh['sub'=16,'row'=16] {'sub','row'}, use_global_device_ids=true, to_apply=%region_19.27 | all-reduce | flops 4096 | bytes 32768 | tf_op jit(solution)/shard_map/psum | solution.py:117
  (231 shorter events, 295.2 us)
Async XLA Ops:
  7.2 47.8 %all-gather.4.cloned.1.call-start = ((), (), s32[]{:S(2)}) async-start(), calls=%async_computation.10 | async-start | bytes 1671168 | tf_op jit(solution)/shard_map/all_gather | solution.py:66
  10.1 341.9 %copy-start.12 = (s32[1024]{0:T(1024)}, s32[1024]{0:T(1024)S(1)}, u32[]{:S(2)}) copy-start(s32[1024]{0:T(1024)S(1)} %pad_clamp_fusion.2) | copy-start | bytes 12292
  11.5 101.5 %reduce-scatter.13.cloned.1.call-start = ((), (), s32[]{:S(2)}) async-start(), calls=%async_computation.11 | async-start | bytes 1671168 | tf_op jit(solution)/shard_map/reduce_scatter | solution.py:73
  12.3 293.5 %copy-start.15 = (s32[1024]{0:T(1024)}, s32[1024]{0:T(1024)S(1)}, u32[]{:S(2)}) copy-start(s32[1024]{0:T(1024)S(1)} %pad_clamp_fusion) | copy-start | bytes 12292
  15.9 190.7 %reduce-scatter.11.cloned.1.call-start = ((), (), s32[]{:S(2)}) async-start(), calls=%async_computation.9 | async-start | bytes 6684672 | tf_op jit(solution)/shard_map/reduce_scatter | solution.py:56
  16.0 298.1 %copy-start.14 = (s32[1024]{0:T(1024)}, s32[1024]{0:T(1024)S(1)}, u32[]{:S(2)}) copy-start(s32[1024]{0:T(1024)S(1)} %pad_clamp_fusion.3) | copy-start | bytes 12292
  39.4 103.6 %all-to-all-start = ((f32[16,768,128]{2,1,0:T(8,128)}), f32[16,768,128]{2,1,0:T(8,128)}, u32[]{:S(2)}, u32[]{:S(2)}) async-start(f32[16,768,128]{2,1,0:T(8,128)} %stack.6), calls=%async_computation | async-start | bytes 12582912 | tf_op jit(solution)/shard_map/all_to_all | solution.py:46
  47.6 65.5 %copy-start.22 = (s32[1,1,3]{2,1,0:T(1,128)S(1)}, s32[1,1,3]{2,1,0:T(1,128)}, u32[]{:S(2)}) copy-start(s32[1,1,3]{2,1,0:T(1,128)} %param.28) | copy-start | bytes 40
  47.6 334.8 %reduce-scatter.19.cloned.1.call-start = ((), (), s32[]{:S(2)}) async-start(), calls=%async_computation.16 | async-start | bytes 1671168 | tf_op jit(solution)/shard_map/reduce_scatter | solution.py:73
  51.0 355.7 %copy-start.13 = (s32[1024]{0:T(1024)}, s32[1024]{0:T(1024)S(1)}, u32[]{:S(2)}) copy-start(s32[1024]{0:T(1024)S(1)} %pad_clamp_fusion.4) | copy-start | bytes 12292
  51.0 326.1 %copy-start.16 = (s32[1024]{0:T(1024)}, s32[1024]{0:T(1024)S(1)}, u32[]{:S(2)}) copy-start(s32[1024]{0:T(1024)S(1)} %pad_clamp_fusion.1) | copy-start | bytes 12292
  153.7 57.6 %copy-start.19 = (s32[1,1,12]{2,1,0:T(1,128)S(1)}, s32[1,1,12]{2,1,0:T(1,128)}, u32[]{:S(2)}) copy-start(s32[1,1,12]{2,1,0:T(1,128)} %param.29) | copy-start | bytes 148
  211.4 93.8 %copy-start.10 = (f32[768]{0:T(1024)S(1)}, f32[768]{0:T(1024)}, u32[]{:S(2)}) copy-start(f32[768]{0:T(1024)} %param.24) | copy-start | bytes 9220
  313.9 143.7 %reduce-scatter.15.cloned.1.call-start = ((), (), s32[]{:S(2)}) async-start(), calls=%async_computation.12 | async-start | bytes 3342336 | tf_op jit(solution)/shard_map/reduce_scatter | solution.py:56
  347.5 53.3 %all-to-all-start.1 = ((f32[16,768,64]{1,2,0:T(8,128)}), f32[16,768,64]{1,2,0:T(8,128)}, u32[]{:S(2)}, u32[]{:S(2)}) async-start(f32[16,768,64]{1,2,0:T(8,128)} %stack.7), calls=%async_computation.3 | async-start | bytes 6291456 | tf_op jit(solution)/shard_map/all_to_all | solution.py:46
  352.0 356.5 %all-reduce.5.cloned.1.call-start = ((), (), s32[]{:S(2)}) async-start(), calls=%async_computation.13 | async-start | bytes 131072 | tf_op jit(solution)/shard_map/psum | solution.py:109
  422.9 42.9 %copy-start.20 = (s32[1,1,12]{2,1,0:T(1,128)S(1)}, s32[1,1,12]{2,1,0:T(1,128)}, u32[]{:S(2)}) copy-start(s32[1,1,12]{2,1,0:T(1,128)} %param.29) | copy-start | bytes 148
  469.1 518.8 %reduce-scatter.21.cloned.1.call-start = ((), (), s32[]{:S(2)}) async-start(), calls=%async_computation.17 | async-start | bytes 1671168 | tf_op jit(solution)/shard_map/reduce_scatter | solution.py:73
  735.9 177.9 %copy-start.18 = (s32[1,1,12]{2,1,0:T(1,128)S(1)}, s32[1,1,12]{2,1,0:T(1,128)}, u32[]{:S(2)}) copy-start(s32[1,1,12]{2,1,0:T(1,128)} %param.30) | copy-start | bytes 148
  919.1 142.0 %reduce-scatter.17.cloned.1.call-start = ((), (), s32[]{:S(2)}) async-start(), calls=%async_computation.14 | async-start | bytes 3342336 | tf_op jit(solution)/shard_map/reduce_scatter | solution.py:56
  952.6 53.3 %all-to-all-start.2 = ((f32[16,768,64]{1,2,0:T(8,128)}), f32[16,768,64]{1,2,0:T(8,128)}, u32[]{:S(2)}, u32[]{:S(2)}) async-start(f32[16,768,64]{1,2,0:T(8,128)} %stack.8), calls=%async_computation.5 | async-start | bytes 6291456 | tf_op jit(solution)/shard_map/all_to_all | solution.py:46
  957.1 351.7 %all-reduce.7.cloned.1.call-start = ((), (), s32[]{:S(2)}) async-start(), calls=%async_computation.15 | async-start | bytes 131072 | tf_op jit(solution)/shard_map/psum | solution.py:109
  1028.1 39.3 %copy-start.4 = (f32[12,64,64]{2,0,1:T(8,128)S(1)}, f32[12,64,64]{2,0,1:T(8,128)}, u32[]{:S(2)}) copy-start(f32[12,64,64]{2,0,1:T(8,128)} %fusion.36) | copy-start | bytes 589828
  1028.1 39.4 %copy-start.21 = (s32[1,1,12]{2,1,0:T(1,128)S(1)}, s32[1,1,12]{2,1,0:T(1,128)}, u32[]{:S(2)}) copy-start(s32[1,1,12]{2,1,0:T(1,128)} %param.29) | copy-start | bytes 148
  (12 other events, 91.9 us)
Sparse Core Ops, SparseCore 0:
  11.7 43.3 all-gather.3
  57.6 55.4 reduce-scatter.12
  117.2 89.2 reduce-scatter.10
  314.0 52.0 reduce-scatter.18
  369.5 87.9 reduce-scatter.14
  469.3 239.1 all-reduce.4
  919.2 50.4 reduce-scatter.20
  973.7 87.2 reduce-scatter.16
  1069.6 239.1 all-reduce.6
